TPU v7x, 512 devices: a whole 4x4x16 slice. The times are simulated.
512 devices in a mesh: row: 16 (over x, z_lo), col: 32 (over z_hi, y, core).
Axes of the slice: x: 4, y: 4, z: 16 (z_hi: 4, z_lo: 4; z = z_hi * 4 + z_lo), core: 2. Of those that a mesh axis runs over, the one named last changes fastest.
Arguments:
- spectra: bfloat16 [2048, 2, 128, 128], P(('row', 'col')), may hold values from -3600 to 3600
- kept_windows: int32 [128], replicated, may hold values 0 or 1
Outputs:
- correlations: float32 [2048, 32, 64, 128], P('row', 'col')
All inputs are finite; a program needn't handle non-finite values.
Results may differ from a plain program's by a relative error of at most 0.0025.
Values may be sent and summed in bfloat16 or wider, within the bound.
A program may use at most 128 MiB of HBM per device.

v0:
```python
import math
import jax
import jax.numpy as jnp
from jax import lax
from jax.sharding import PartitionSpec as P

EPSILON = 1e-06


def make_lag_table(bins_count, windows):
    bin_ids = jnp.arange(bins_count, dtype=jnp.int32)
    phase_index = bin_ids[:, None] * bin_ids[None, :] % bins_count
    phases = phase_index.astype(jnp.float32) * (2.0 * math.pi / bins_count)
    norming = 1.0 / math.sqrt(bins_count * windows)
    return jnp.stack([jnp.cos(phases) * norming, -jnp.sin(phases) * norming], axis=1)


def partner_operand(col_rows):
    real_part = col_rows[:, 0]
    imag_part = col_rows[:, 1]
    re_half = jnp.concatenate([real_part, imag_part], axis=2)
    im_half = jnp.concatenate([-imag_part, real_part], axis=2)
    return jnp.concatenate([re_half, im_half], axis=0)


def cross_lags(first_rows, partner, lag_table):
    first_half = jnp.concatenate([first_rows[:, 0], first_rows[:, 1]], axis=2)
    stacks = lax.dot_general(
        first_half, partner, (((2,), (2,)), ((1,), (1,))), preferred_element_type=jnp.float32
    )
    partners_count = partner.shape[0] // 2
    stacks = stacks.reshape(stacks.shape[0], stacks.shape[1], 2, partners_count)
    return jnp.einsum("fmps,fpk->msk", stacks, lag_table, precision=lax.Precision.HIGHEST)


def body(spectra, kept_windows):
    bins_count = spectra.shape[2]
    windows = spectra.shape[3]
    own_float = spectra.astype(jnp.float32)
    partial_energy = jnp.sum(own_float * own_float, axis=(0, 1, 2))
    channels = spectra.shape[0] * lax.axis_size("row") * lax.axis_size("col")
    energy_sum = lax.psum(partial_energy, ("row", "col"))
    energy = energy_sum / (channels * 2 * bins_count) + EPSILON
    factor = kept_windows.astype(jnp.float32) / energy
    column_block = lax.all_gather(spectra, "row", axis=0, tiled=True)
    partner = partner_operand(column_block)
    lag_table = make_lag_table(bins_count, windows)
    row_block = lax.all_gather(spectra, "col", axis=0, tiled=True)
    lag_rows = cross_lags(
        (row_block.astype(jnp.float32) * factor).astype(jnp.bfloat16), partner, lag_table
    )
    return lag_rows[:, None]


def solution(mesh):
    placed = (P(("row", "col"), None, None, None), P())
    return jax.shard_map(
        body, mesh=mesh, in_specs=placed, out_specs=P("row", "col", None, None), check_vma=False
    )
```

profile of v0, /device:TPU:1, one launch (start us, length us, event | category | flops | bytes accessed | tf_op | source)
XLA Modules:
  0.0 314.2 jit_solution(12809178669511933960)
XLA Ops:
  6.5 0.0 all-gather.5.cloned.1.call-start
  6.5 0.7 all-gather.5.cloned.1.call-update
  7.3 0.0 all-gather.3.cloned.1.call-start
  7.3 0.7 all-gather.3.cloned.1.call-update
  8.0 1.1 multiply_reduce_fusion
  9.1 112.5 %psum.7 = f32[128]{0:T(128)S(1)} all-reduce(f32[128]{0:T(128)S(1)} %multiply_reduce_fusion), channel_id=1, replica_groups=mesh['row'=16,'col'=32] {'row','col'}, use_global_device_ids=true, to_apply=%region_1.0 | all-reduce | flops 128 | bytes 1024 | tf_op jit(solution)/shard_map/psum | solution.py:42
  121.6 0.3 negate_multiply_fusion
  121.9 0.7 add_divide_fusion
  122.6 1.0 all-gather.5.cloned.1.call-done
  123.6 2.7 fusion.27
  126.3 2.9 fusion.26
  129.3 4.6 %copy_bitcast_fusion = (bf16[64,128,128]{2,0,1:T(8,128)(2,1)}, bf16[64,128,128]{2,0,1:T(8,128)(2,1)}) fusion(bf16[64,1,128,128]{3,2,1,0:T(8,128)(2,1)S(1)} %get-tuple-element.7, bf16[64,1,128,128]{3,2,1,0:T(8,128)(2,1)S(1)} %get-tuple-element.8), kind=kLoop, calls=%fused_computation.17 | loop fusion | bytes 8388608 | tf_op jit(solution)/shard_map/squeeze | solution.py:20
  133.9 126.8 %all-gather.3.cloned.1.call-done = bf16[128,2,128,128]{3,2,1,0:T(8,128)(2,1)} async-done(((bf16[4,2,128,128]{3,2,1,0:T(8,128)(2,1)}), bf16[128,2,128,128]{3,2,1,0:T(8,128)(2,1)}) %all-gather.3.cloned.1.call-update) | async-done | bytes 8388624 | tf_op jit(solution)/shard_map/all_gather | solution.py:48
  260.7 12.0 %multiply_convert_fusion = bf16[128,2,128,128]{3,0,2,1:T(8,128)(2,1)} fusion(bf16[128,2,128,128]{3,2,1,0:T(8,128)(2,1)} %all-gather.3.cloned.1.call-done, f32[128]{0:T(128)S(1)} %add_divide_fusion), kind=kLoop, calls=%fused_computation | loop fusion | flops 12582912 | bytes 16777728 | tf_op jit(solution)/shard_map/convert_element_type | solution.py:50
  272.8 6.1 %slice_bitcast_fusion.1 = (bf16[128,128,128]{2,0,1:T(8,128)(2,1)}, bf16[128,128,128]{2,0,1:T(8,128)(2,1)}) fusion(bf16[128,2,128,128]{3,0,2,1:T(8,128)(2,1)} %multiply_convert_fusion), kind=kLoop, calls=%fused_computation.15 | loop fusion | bytes 16777216 | tf_op jit(solution)/shard_map/squeeze | solution.py:27
  278.9 7.1 %fusion = f32[128,128,128]{1,2,0:T(8,128)S(1)} fusion(bf16[128,128,128]{2,0,1:T(8,128)(2,1)} %get-tuple-element.6, bf16[128,128,128]{2,0,1:T(8,128)(2,1)} %get-tuple-element.5, bf16[64,128,128]{2,0,1:T(8,128)(2,1)} %get-tuple-element.10, bf16[64,128,128]{2,0,1:T(8,128)(2,1)} %fusion.26, bf16[64,128,128]{2,0,1:T(8,128)(2,1)} %get-tuple-element.9), kind=kOutput, calls=%fused_computation.1 | convolution fusion | flops 1124073472 | bytes 23068672 | tf_op jit(solution)/shard_map/dot_general | solution.py:28
  286.0 16.9 %fusion.13 = f32[128,1,64,128]{3,0,2,1:T(8,128)S(1)} fusion(f32[128,128,2,64]{1,3,2,0:T(8,128)S(1)} %bitcast.18, f32[128,1,128]{2,0,1:T(8,128)S(1)} %get-tuple-element.11, f32[128,1,128]{2,0,1:T(8,128)S(1)} %get-tuple-element.12), kind=kOutput, calls=%fused_computation.16 | convolution fusion | flops 3221258240 | bytes 12713984 | tf_op jit(solution)/shard_map/fmps,fpk->msk/dot_general | solution.py:33
  302.9 4.4 %copy.11 = f32[128,1,64,128]{3,2,1,0:T(8,128)} copy(f32[128,1,64,128]{3,0,2,1:T(8,128)S(1)} %fusion.13) | data formatting | bytes 8388608 | tf_op jit(solution)/shard_map/broadcast_in_dim | solution.py:52
Async XLA Ops:
  6.5 117.1 %all-gather.5.cloned.1.call-start = ((), (), s32[]{:S(2)}) async-start(), calls=%async_computation.1 | async-start | bytes 4456448 | tf_op jit(solution)/shard_map/all_gather | solution.py:45
  7.3 253.5 %all-gather.3.cloned.1.call-start = ((), (), s32[]{:S(2)}) async-start(), calls=%async_computation | async-start | bytes 8650752 | tf_op jit(solution)/shard_map/all_gather | solution.py:48
Sparse Core Ops, SparseCore 0:
  9.4 114.1 all-gather.4
  126.7 133.9 all-gather.2
where the time goes:
time: 314 us
  waiting for transfers between devices  129 us (41%)
  blocking collectives  113 us (36%)
  matrix products  24 us (8%)
  local copies, waits for them, and re-layouts  17.9 us (6%)
  other arithmetic  17 us (5%)
  between operations  13.4 us (4%)
    all_gather x1, waiting for transfers between devices, body(): row_block = lax.all_gather(spectra, 'col', axis=0, tiled=True)  127 us
    psum x1, blocking collectives, body(): energy_sum = lax.psum(partial_energy, ('row', 'col'))  113 us
    dot_general x1, matrix products, cross_lags(): jnp.einsum('fmps,fpk->msk', stacks, lag_table, precision=lax.Precision.HI...  16.9 us
    convert_element_type x1, other arithmetic, body(): (row_block.astype(jnp.float32) * factor).astype(jnp.bfloat16)  12 us
    dot_general x1, matrix products, cross_lags(): lax.dot_general(first_half, partner, (((2,), (2,)), ((1,), (1,))), prefer...  7.12 us
  transfers between devices with their start and end apart: 2, of which 2 were waited for; matrix products, arithmetic and copies ran while one was open for 4% of the time, Pallas kernels for 0%

commit v1 on v0

--- a/solution.py
+++ b/solution.py
@@ -45,7 +45,8 @@
     column_block = lax.all_gather(spectra, "row", axis=0, tiled=True)
     partner = partner_operand(column_block)
     lag_table = make_lag_table(bins_count, windows)
-    row_block = lax.all_gather(spectra, "col", axis=0, tiled=True)
+    stack = jnp.stack([spectra] * lax.axis_size("col"))
+    row_block = jnp.concatenate(lax.all_to_all(stack, "col", 0, 0), axis=0)
     lag_rows = cross_lags(
         (row_block.astype(jnp.float32) * factor).astype(jnp.bfloat16), partner, lag_table
     )

time: 314 us -> 654 us (2.08)
  blocking collectives: 113 us -> 518 us
  waiting for transfers between devices: 129 us -> 0.7 us
  other arithmetic: 17 us -> 41.5 us
  starting transfers between devices: 0.04 us -> 19.6 us
  local copies, waits for them, and re-layouts: 17.9 us -> 33.1 us
    psum x1, blocking collectives: 113 us -> 518 us  [body(): energy_sum = lax.psum(partial_energy, ('row', 'col'))]
    all_gather x1 -> x0, waiting for transfers between devices: 127 us -> none  [body(): row_block = lax.all_gather(spectra, 'col', axis=0, tiled=True)]
    all_to_all x0 -> x1, starting transfers between devices: none -> 19.6 us  [body(): row_block = jnp.concatenate(lax.all_to_all(stack, 'col', 0, 0), axis=0)]
    convert_element_type x1, other arithmetic: 12 us -> 26.9 us  [body(): (row_block.astype(jnp.float32) * factor).astype(jnp.bfloat16)]
    convert_element_type x0 -> x1, other arithmetic: none -> 11.2 us  [body(): row_block.astype(jnp.float32) * factor]
    all_to_all x0 -> x1, local copies, waits for them, and re-layouts: none -> 8.97 us  [body(): row_block = jnp.concatenate(lax.all_to_all(stack, 'col', 0, 0), axis=0)]
    another operation x0 -> x1, local copies, waits for them, and re-layouts: none -> 7.27 us  [body(): stack = jnp.stack([spectra] * lax.axis_size('col'))]
  transfers between devices with their start and end apart: 2 -> 2, of which waited for: 2 -> 0; matrix products, arithmetic and copies ran while one was open for 4% -> 2% of each run, Pallas kernels for 0% -> 0%
where the time goes in v1:
time: 654 us; the launch traced here: 651 us
  blocking collectives  518 us (79%)
  other arithmetic  41.5 us (6%)
  local copies, waits for them, and re-layouts  33.1 us (5%)
  matrix products  24 us (4%)
  starting transfers between devices  19.6 us (3%)
  between operations  13.7 us (2%)
    psum x1, blocking collectives, body(): energy_sum = lax.psum(partial_energy, ('row', 'col'))  518 us
    convert_element_type x1, other arithmetic, body(): (row_block.astype(jnp.float32) * factor).astype(jnp.bfloat16)  26.9 us
    all_to_all x1, starting transfers between devices, body(): row_block = jnp.concatenate(lax.all_to_all(stack, 'col', 0, 0), axis=0)  19.6 us
    dot_general x1, matrix products, cross_lags(): jnp.einsum('fmps,fpk->msk', stacks, lag_table, precision=lax.Precision.HI...  16.9 us
  transfers between devices with their start and end apart: 2, of which 0 were waited for; matrix products, arithmetic and copies ran while one was open for 2% of the time, Pallas kernels for 0%

profile of v1, /device:TPU:1, one launch (start us, length us, event | category | flops | bytes accessed | tf_op | source)
XLA Modules:
  0.0 650.9 jit_solution(10861820942700473595)
XLA Ops:
  6.5 1.2 copy.13
  7.7 7.3 %stack.4 = bf16[32,4,2,128,128]{4,1,3,2,0:T(4,128)(2,1)} broadcast(bf16[4,2,128,128]{3,0,2,1:T(4,128)(2,1)S(1)} %copy.13), dimensions={1,2,3,4} | broadcast | bytes 8650752 | tf_op jit(solution)/shard_map/stack | solution.py:48
  15.0 0.0 copy-start
  15.0 0.0 copy-start.1
  15.0 19.6 %all-to-all-start = ((bf16[32,4,2,128,128]{4,1,3,2,0:T(4,128)(2,1)}), bf16[32,4,2,128,128]{4,1,3,2,0:T(4,128)(2,1)}, u32[]{:S(2)}, u32[]{:S(2)}) async-start(bf16[32,4,2,128,128]{4,1,3,2,0:T(4,128)(2,1)} %stack.4), calls=%async_computation | async-start | bytes 16777216 | tf_op jit(solution)/shard_map/all_to_all | solution.py:49
  34.5 0.0 all-gather.2.cloned.1.call-start
  34.6 0.7 all-gather.2.cloned.1.call-update
  35.3 0.0 copy-done
  35.3 0.2 multiply_reduce_fusion
  35.4 518.3 %psum.7 = f32[128]{0:T(128)S(1)} all-reduce(f32[128]{0:T(128)S(1)} %multiply_reduce_fusion), channel_id=1, replica_groups=mesh['row'=16,'col'=32] {'row','col'}, use_global_device_ids=true, to_apply=%region_1.0 | all-reduce | flops 128 | bytes 1024 | tf_op jit(solution)/shard_map/psum | solution.py:42
  553.7 0.3 negate_multiply_fusion
  554.0 0.0 copy-done.1
  554.0 0.0 all-gather.2.cloned.1.call-done
  554.1 2.7 fusion.28
  556.8 2.9 fusion.27
  559.7 4.7 copy_bitcast_fusion
  564.4 0.0 all-to-all-done
  564.4 9.0 %copy.14 = bf16[32,4,2,128,128]{4,3,2,1,0:T(8,128)(2,1)} copy(bf16[32,4,2,128,128]{4,1,3,2,0:T(4,128)(2,1)} %all-to-all-done) | data formatting | bytes 16777216 | tf_op jit(solution)/shard_map/all_to_all | solution.py:49
  573.4 11.2 %bitcast_convert_fusion = f32[128,2,128,128]{3,2,1,0:T(8,128)} fusion(bf16[32,4,2,128,128]{4,3,2,1,0:T(8,128)(2,1)} %copy.14), kind=kLoop, calls=%fused_computation.13 | loop fusion | flops 4194304 | bytes 25165824 | tf_op jit(solution)/shard_map/convert_element_type | solution.py:51
  584.6 26.9 %fusion = bf16[128,2,128,128]{3,0,2,1:T(8,128)(2,1)S(1)} fusion(f32[128,2,128,128]{3,2,1,0:T(8,128)} %bitcast_convert_fusion, f32[128]{0:T(128)S(1)} %add_divide_fusion), kind=kLoop, calls=%fused_computation.1 | loop fusion | flops 8388608 | bytes 25166336 | tf_op jit(solution)/shard_map/convert_element_type | solution.py:51
  611.5 3.9 slice_bitcast_fusion.1
  615.4 7.1 %fusion.1 = f32[128,128,128]{1,2,0:T(8,128)S(1)} fusion(bf16[128,128,128]{2,0,1:T(8,128)(2,1)} %get-tuple-element.6, bf16[128,128,128]{2,0,1:T(8,128)(2,1)} %get-tuple-element.5, bf16[64,128,128]{2,0,1:T(8,128)(2,1)} %get-tuple-element.10, bf16[64,128,128]{2,0,1:T(8,128)(2,1)} %fusion.27, bf16[64,128,128]{2,0,1:T(8,128)(2,1)} %get-tuple-element.9), kind=kOutput, calls=%fused_computation.2 | convolution fusion | flops 1124073472 | bytes 23068672 | tf_op jit(solution)/shard_map/dot_general | solution.py:28
  622.5 16.9 %fusion.14 = f32[128,1,64,128]{3,0,2,1:T(8,128)S(1)} fusion(f32[128,128,2,64]{1,3,2,0:T(8,128)S(1)} %bitcast.21, f32[128,1,128]{2,0,1:T(8,128)S(1)} %get-tuple-element.11, f32[128,1,128]{2,0,1:T(8,128)S(1)} %get-tuple-element.12), kind=kOutput, calls=%fused_computation.18 | convolution fusion | flops 3221258240 | bytes 12713984 | tf_op jit(solution)/shard_map/fmps,fpk->msk/dot_general | solution.py:33
  639.4 4.4 copy.19
  (1 shorter events, 0.0 us)
Async XLA Ops:
  15.0 20.3 %copy-start = (bf16[4,2,128,128]{3,2,1,0:T(8,128)(2,1)S(1)}, bf16[4,2,128,128]{3,2,1,0:T(8,128)(2,1)}, u32[]{:S(2)}) copy-start(bf16[4,2,128,128]{3,2,1,0:T(8,128)(2,1)} %param.2) | copy-start | bytes 786436
  15.0 539.0 %copy-start.1 = (s32[128]{0:T(128)S(1)}, s32[128]{0:T(128)}, u32[]{:S(2)}) copy-start(s32[128]{0:T(128)} %param.3) | copy-start | bytes 1540
  15.0 549.4 %all-to-all-start = ((bf16[32,4,2,128,128]{4,1,3,2,0:T(4,128)(2,1)}), bf16[32,4,2,128,128]{4,1,3,2,0:T(4,128)(2,1)}, u32[]{:S(2)}, u32[]{:S(2)}) async-start(bf16[32,4,2,128,128]{4,1,3,2,0:T(4,128)(2,1)} %stack.4), calls=%async_computation | async-start | bytes 16777216 | tf_op jit(solution)/shard_map/all_to_all | solution.py:49
  34.5 519.5 %all-gather.2.cloned.1.call-start = ((), (), s32[]{:S(2)}) async-start(), calls=%async_computation.1 | async-start | bytes 4456448 | tf_op jit(solution)/shard_map/all_gather | solution.py:45
Sparse Core Ops, SparseCore 0:
  37.5 370.5 all-gather.1

commit v2 on v0

--- a/solution.py
+++ b/solution.py
@@ -39,7 +39,8 @@
     own_float = spectra.astype(jnp.float32)
     partial_energy = jnp.sum(own_float * own_float, axis=(0, 1, 2))
     channels = spectra.shape[0] * lax.axis_size("row") * lax.axis_size("col")
-    energy_sum = lax.psum(partial_energy, ("row", "col"))
+    half = lax.psum(partial_energy, "row")
+    energy_sum = lax.psum(half, "col")
     energy = energy_sum / (channels * 2 * bins_count) + EPSILON
     factor = kept_windows.astype(jnp.float32) / energy
     column_block = lax.all_gather(spectra, "row", axis=0, tiled=True)

time: 314 us -> 314 us (level)
  waiting for transfers between devices: 129 us -> 107 us
  blocking collectives: 113 us -> 134 us
    psum x1 -> x2, blocking collectives: 113 us -> 134 us  [the longest x1 94.9 us: body(): energy_sum = lax.psum(half, 'col')]
    all_gather x1, waiting for transfers between devices: 127 us -> 106 us  [body(): row_block = lax.all_gather(spectra, 'col', axis=0, tiled=True)]
  transfers between devices with their start and end apart: 2 -> 2, of which waited for: 2 -> 1; matrix products, arithmetic and copies ran while one was open for 4% -> 4% of each run, Pallas kernels for 0% -> 0%
where the time goes in v2:
time: 314 us
  blocking collectives  134 us (43%)
  waiting for transfers between devices  107 us (34%)
  matrix products  24.2 us (8%)
  local copies, waits for them, and re-layouts  17.9 us (6%)
  other arithmetic  17 us (5%)
  between operations  13.4 us (4%)
    all_gather x1, waiting for transfers between devices, body(): row_block = lax.all_gather(spectra, 'col', axis=0, tiled=True)  106 us
    psum x1, blocking collectives, body(): energy_sum = lax.psum(half, 'col')  94.9 us
    psum x1, blocking collectives, body(): half = lax.psum(partial_energy, 'row')  39.4 us
    dot_general x1, matrix products, cross_lags(): jnp.einsum('fmps,fpk->msk', stacks, lag_table, precision=lax.Precision.HI...  16.9 us
    convert_element_type x1, other arithmetic, body(): (row_block.astype(jnp.float32) * factor).astype(jnp.bfloat16)  12 us
    dot_general x1, matrix products, cross_lags(): lax.dot_general(first_half, partner, (((2,), (2,)), ((1,), (1,))), prefer...  7.28 us
  transfers between devices with their start and end apart: 2, of which 1 were waited for; matrix products, arithmetic and copies ran while one was open for 4% of the time, Pallas kernels for 0%

profile of v2, /device:TPU:1, one launch (start us, length us, event | category | flops | bytes accessed | tf_op | source)
XLA Modules:
  0.0 314.0 jit_solution(16224193166396196249)
XLA Ops:
  6.5 0.0 all-gather.5.cloned.1.call-start
  6.5 0.7 all-gather.5.cloned.1.call-update
  7.3 0.0 all-gather.3.cloned.1.call-start
  7.3 0.7 all-gather.3.cloned.1.call-update
  8.0 1.1 multiply_reduce_fusion
  9.1 39.4 %psum.14 = f32[128]{0:T(128)S(1)} all-reduce(f32[128]{0:T(128)S(1)} %multiply_reduce_fusion), channel_id=1, replica_groups=mesh['row'=16,'col'=32] {'row'}, use_global_device_ids=true, to_apply=%region_1.0 | all-reduce | flops 128 | bytes 1024 | tf_op jit(solution)/shard_map/psum | solution.py:42
  48.5 94.9 %psum.15 = f32[128]{0:T(128)S(1)} all-reduce(f32[128]{0:T(128)S(1)} %psum.14), channel_id=1, replica_groups=mesh['row'=16,'col'=32] {'col'}, use_global_device_ids=true, to_apply=%region_2.0 | all-reduce | flops 128 | bytes 1024 | tf_op jit(solution)/shard_map/psum | solution.py:43
  143.4 0.3 negate_multiply_fusion
  143.7 0.7 add_divide_fusion
  144.3 0.0 all-gather.5.cloned.1.call-done
  144.3 2.7 fusion.27
  147.1 2.9 fusion.26
  150.0 4.6 %copy_bitcast_fusion = (bf16[64,128,128]{2,0,1:T(8,128)(2,1)}, bf16[64,128,128]{2,0,1:T(8,128)(2,1)}) fusion(bf16[64,1,128,128]{3,2,1,0:T(8,128)(2,1)S(1)} %get-tuple-element.7, bf16[64,1,128,128]{3,2,1,0:T(8,128)(2,1)S(1)} %get-tuple-element.8), kind=kLoop, calls=%fused_computation.17 | loop fusion | bytes 8388608 | tf_op jit(solution)/shard_map/squeeze | solution.py:20
  154.6 105.7 %all-gather.3.cloned.1.call-done = bf16[128,2,128,128]{3,2,1,0:T(8,128)(2,1)} async-done(((bf16[4,2,128,128]{3,2,1,0:T(8,128)(2,1)}), bf16[128,2,128,128]{3,2,1,0:T(8,128)(2,1)}) %all-gather.3.cloned.1.call-update) | async-done | bytes 8388624 | tf_op jit(solution)/shard_map/all_gather | solution.py:49
  260.4 12.0 %multiply_convert_fusion = bf16[128,2,128,128]{3,0,2,1:T(8,128)(2,1)} fusion(bf16[128,2,128,128]{3,2,1,0:T(8,128)(2,1)} %all-gather.3.cloned.1.call-done, f32[128]{0:T(128)S(1)} %add_divide_fusion), kind=kLoop, calls=%fused_computation | loop fusion | flops 12582912 | bytes 16777728 | tf_op jit(solution)/shard_map/convert_element_type | solution.py:51
  272.4 6.1 %slice_bitcast_fusion.1 = (bf16[128,128,128]{2,0,1:T(8,128)(2,1)}, bf16[128,128,128]{2,0,1:T(8,128)(2,1)}) fusion(bf16[128,2,128,128]{3,0,2,1:T(8,128)(2,1)} %multiply_convert_fusion), kind=kLoop, calls=%fused_computation.15 | loop fusion | bytes 16777216 | tf_op jit(solution)/shard_map/squeeze | solution.py:27
  278.5 7.3 %fusion = f32[128,128,128]{1,2,0:T(8,128)S(1)} fusion(bf16[128,128,128]{2,0,1:T(8,128)(2,1)} %get-tuple-element.6, bf16[128,128,128]{2,0,1:T(8,128)(2,1)} %get-tuple-element.5, bf16[64,128,128]{2,0,1:T(8,128)(2,1)} %get-tuple-element.10, bf16[64,128,128]{2,0,1:T(8,128)(2,1)} %fusion.26, bf16[64,128,128]{2,0,1:T(8,128)(2,1)} %get-tuple-element.9), kind=kOutput, calls=%fused_computation.1 | convolution fusion | flops 1124073472 | bytes 23068672 | tf_op jit(solution)/shard_map/dot_general | solution.py:28
  285.8 16.9 %fusion.13 = f32[128,1,64,128]{3,0,2,1:T(8,128)S(1)} fusion(f32[128,128,2,64]{1,3,2,0:T(8,128)S(1)} %bitcast.18, f32[128,1,128]{2,0,1:T(8,128)S(1)} %get-tuple-element.11, f32[128,1,128]{2,0,1:T(8,128)S(1)} %get-tuple-element.12), kind=kOutput, calls=%fused_computation.16 | convolution fusion | flops 3221258240 | bytes 12713984 | tf_op jit(solution)/shard_map/fmps,fpk->msk/dot_general | solution.py:33
  302.7 4.4 %copy.11 = f32[128,1,64,128]{3,2,1,0:T(8,128)} copy(f32[128,1,64,128]{3,0,2,1:T(8,128)S(1)} %fusion.13) | data formatting | bytes 8388608 | tf_op jit(solution)/shard_map/broadcast_in_dim | solution.py:53
Async XLA Ops:
  6.5 137.8 %all-gather.5.cloned.1.call-start = ((), (), s32[]{:S(2)}) async-start(), calls=%async_computation.1 | async-start | bytes 4456448 | tf_op jit(solution)/shard_map/all_gather | solution.py:46
  7.3 253.1 %all-gather.3.cloned.1.call-start = ((), (), s32[]{:S(2)}) async-start(), calls=%async_computation | async-start | bytes 8650752 | tf_op jit(solution)/shard_map/all_gather | solution.py:49
Sparse Core Ops, SparseCore 0:
  9.4 114.7 all-gather.4
  127.4 132.9 all-gather.2

commit v3 on v0

--- a/solution.py
+++ b/solution.py
@@ -5,6 +5,11 @@
 from jax.sharding import PartitionSpec as P
 
 EPSILON = 1e-06
+
+
+def add_all(block, name):
+    terms = lax.all_gather(block, name)
+    return jnp.sum(terms, axis=0)
 
 
 def make_lag_table(bins_count, windows):
@@ -39,7 +44,7 @@
     own_float = spectra.astype(jnp.float32)
     partial_energy = jnp.sum(own_float * own_float, axis=(0, 1, 2))
     channels = spectra.shape[0] * lax.axis_size("row") * lax.axis_size("col")
-    energy_sum = lax.psum(partial_energy, ("row", "col"))
+    energy_sum = add_all(partial_energy, ("row", "col"))
     energy = energy_sum / (channels * 2 * bins_count) + EPSILON
     factor = kept_windows.astype(jnp.float32) / energy
     column_block = lax.all_gather(spectra, "row", axis=0, tiled=True)

time: 314 us -> 890 us (2.83)
  the two profiles are of different devices: /device:TPU:1 before, /device:TPU:35 now
where the time goes in v3:
time: 890 us; the launch traced here: 881 us
  blocking collectives  794 us (89%)
  other arithmetic  29.5 us (3%)
  matrix products  24 us (3%)
  local copies, waits for them, and re-layouts  17.9 us (2%)
  between operations  13.8 us (2%)
    all_gather x1, blocking collectives, add_all(): terms = lax.all_gather(block, name)  794 us
    convert_element_type x1, other arithmetic, body(): (row_block.astype(jnp.float32) * factor).astype(jnp.bfloat16)  23.9 us
  transfers between devices with their start and end apart: 2, of which 0 were waited for; matrix products, arithmetic and copies ran while one was open for 1% of the time, Pallas kernels for 0%

profile of v3, /device:TPU:35, one launch (start us, length us, event | category | flops | bytes accessed | tf_op | source)
XLA Modules:
  0.0 880.8 jit_solution(14841206751318089038)
XLA Ops:
  6.5 0.0 all-gather.7.cloned.1.call-start
  6.5 0.7 all-gather.7.cloned.1.call-update
  7.3 0.0 all-gather.5.cloned.1.call-start
  7.3 0.7 all-gather.5.cloned.1.call-update
  8.0 1.1 multiply_reduce_fusion
  9.1 794.2 %all-gather.1 = f32[512,1,128]{2,1,0:T(1,128)S(1)} all-gather(f32[1,1,128]{2,1,0:T(1,128)S(1)} %bitcast.20), channel_id=2, replica_groups=mesh['row'=16,'col'=32] {'row','col'}, dimensions={0}, use_global_device_ids=true | all-gather | bytes 262656 | tf_op jit(solution)/shard_map/all_gather | solution.py:11
  803.3 0.6 reduce_sum.19
  803.8 0.3 negate_multiply_fusion
  804.1 0.7 add_divide_fusion
  804.8 0.0 all-gather.7.cloned.1.call-done
  804.8 2.7 fusion.27
  807.5 2.9 fusion.26
  810.5 4.6 copy_bitcast_fusion
  815.1 0.0 all-gather.5.cloned.1.call-done
  815.1 23.9 %multiply_convert_fusion = bf16[128,2,128,128]{3,0,2,1:T(8,128)(2,1)} fusion(bf16[128,2,128,128]{3,2,1,0:T(8,128)(2,1)} %all-gather.5.cloned.1.call-done, f32[128]{0:T(128)S(1)} %add_divide_fusion), kind=kLoop, calls=%fused_computation | loop fusion | flops 12582912 | bytes 16777728 | tf_op jit(solution)/shard_map/convert_element_type | solution.py:55
  839.0 6.1 slice_bitcast_fusion.1
  845.2 7.1 fusion
  852.3 16.9 %fusion.13 = f32[128,1,64,128]{3,0,2,1:T(8,128)S(1)} fusion(f32[128,128,2,64]{1,3,2,0:T(8,128)S(1)} %bitcast.19, f32[128,1,128]{2,0,1:T(8,128)S(1)} %get-tuple-element.11, f32[128,1,128]{2,0,1:T(8,128)S(1)} %get-tuple-element.12), kind=kOutput, calls=%fused_computation.16 | convolution fusion | flops 3221258240 | bytes 12713984 | tf_op jit(solution)/shard_map/fmps,fpk->msk/dot_general | solution.py:38
  869.2 4.4 copy.11
Async XLA Ops:
  6.5 798.2 %all-gather.7.cloned.1.call-start = ((), (), s32[]{:S(2)}) async-start(), calls=%async_computation.1 | async-start | bytes 4456448 | tf_op jit(solution)/shard_map/all_gather | solution.py:50
  7.3 807.8 %all-gather.5.cloned.1.call-start = ((), (), s32[]{:S(2)}) async-start(), calls=%async_computation | async-start | bytes 8650752 | tf_op jit(solution)/shard_map/all_gather | solution.py:53
Sparse Core Ops, SparseCore 0:
  9.4 107.3 all-gather.6
  120.0 111.7 all-gather.4
